TPU v7x, 32 devices: a whole 2x2x4 slice. The times are simulated.
32 devices in a mesh: row: 8 (over y, x, core), col: 4 (over z).
Axes of the slice: x: 2, y: 2, z: 4, core: 2. Of those that a mesh axis runs over, the one named last changes fastest.
Arguments:
- traces: bfloat16 [4096, 782], P(('row', 'col')), may hold values from -60 to 60
- taps: float32 [16], replicated, may hold values from -1.5 to 1.5
Outputs:
- correlations: float32 [32, 4096, 4096], P(None, 'row', 'col')
All inputs are finite; a program needn't handle non-finite values.
Results may differ from a plain program's by a relative error of at most 0.0036.
Values may be sent and summed in bfloat16 or wider, within the bound.
A program may use at most 256 MiB of HBM per device.

v0:
```python
import math
import jax
import jax.numpy as jnp
from jax import lax
from jax.sharding import PartitionSpec as P

LAGS = 32


def from_root(array, axis, root):
    mine = lax.axis_index(axis) == root
    return lax.psum(jnp.where(mine, array, jnp.zeros_like(array)), axis)


def whiten(traces, taps, count):
    samples = traces.astype(jnp.float32)
    decimated = jnp.zeros((samples.shape[0], count), jnp.float32)
    for k in range(taps.shape[0]):
        decimated = decimated + taps[k] * samples[:, k : k + 2 * count - 1 : 2]
    centred = decimated - jnp.mean(decimated, axis=1, keepdims=True)
    spread = jnp.sqrt(jnp.mean(centred * centred, axis=1, keepdims=True) + 1e-06)
    return (centred / spread).astype(jnp.bfloat16)


def on_device(traces, taps):
    count = (traces.shape[1] - taps.shape[0] + 2) // 2
    factor = lax.axis_size("row") // lax.axis_size("col")
    column = lax.axis_index("col")
    source = lax.all_gather(traces, "col", axis=0, tiled=True)
    first_block = whiten(source, taps, count)
    pieces = [from_root(source, "row", factor * column + k) for k in range(factor)]
    second_block = jnp.concatenate(pieces, axis=0)
    second_block = whiten(second_block, taps, count)
    lag_count = LAGS
    width = count - lag_count + 1
    scale_factor = 1.0 / math.sqrt(width)
    left = first_block[:, :width]
    groups = []
    for group in range(lag_count // 8):
        shifted = jnp.stack(
            [second_block[:, group * 8 + lag : group * 8 + lag + width] for lag in range(8)], axis=0
        )
        product = jnp.einsum("in,ljn->lij", left, shifted, preferred_element_type=jnp.float32)
        groups.append(product * scale_factor)
    return jnp.concatenate(groups, axis=0)


def solution(mesh):
    placed = (P(("row", "col"), None), P())
    return jax.shard_map(
        on_device, mesh=mesh, in_specs=placed, out_specs=P(None, "row", "col"), check_vma=False
    )
```

profile of v0, /device:TPU:0, one launch (start us, length us, event | category | flops | bytes accessed | tf_op | source)
XLA Modules:
  0.0 332.4 jit_solution(4783237983157764529)
XLA Ops:
  6.5 20.8 %all_gather.3 = bf16[512,782]{0,1:T(8,128)(2,1)S(1)} all-gather(bf16[128,782]{0,1:T(8,128)(2,1)} %param.2), channel_id=1, replica_groups=mesh['row'=8,'col'=4] {'col'}, dimensions={0}, use_global_device_ids=true | all-gather | bytes 1000960 | tf_op jit(solution)/shard_map/all_gather | solution.py:29
  68.9 15.6 %fusion.37 = (f32[512]{0:T(512)S(1)}, f32[512,384]{0,1:T(8,128)S(1)}) fusion(f32[512,384]{0,1:T(8,128)} %slice.314, f32[]{:T(128)} %bitcast.15, f32[512,384]{0,1:T(8,128)} %slice.313, f32[]{:T(128)} %bitcast.14, f32[512,384]{0,1:T(8,128)} %slice.312, f32[]{:T(128)} %bitcast.13, f32[512,384]{0,1:T(8,128)} %slice.311, f32[]{:T(128)} %bitcast.12, ...), kind=kLoop, calls=%fused_computation.88 | loop fusion | flops 6290944 | bytes 13371456 | tf_op jit(solution)/shard_map/reduce_sum | solution.py:20
  88.7 4.3 %slice.290 = f32[1024,384]{0,1:T(8,128)} slice(f32[1024,782]{0,1:T(8,128)S(1)} %maximum_convert_fusion), slice={[0:1024:1], [15:782:2]} | slice | bytes 3145728 | tf_op jit(solution)/shard_map/slice | solution.py:19
  93.0 4.3 %slice.288 = f32[1024,384]{0,1:T(8,128)} slice(f32[1024,782]{0,1:T(8,128)S(1)} %maximum_convert_fusion), slice={[0:1024:1], [14:781:2]} | slice | bytes 3145728 | tf_op jit(solution)/shard_map/slice | solution.py:19
  97.3 4.3 %slice.286 = f32[1024,384]{0,1:T(8,128)} slice(f32[1024,782]{0,1:T(8,128)S(1)} %maximum_convert_fusion), slice={[0:1024:1], [13:780:2]} | slice | bytes 3145728 | tf_op jit(solution)/shard_map/slice | solution.py:19
  101.6 4.3 %slice.284 = f32[1024,384]{0,1:T(8,128)} slice(f32[1024,782]{0,1:T(8,128)S(1)} %maximum_convert_fusion), slice={[0:1024:1], [12:779:2]} | slice | bytes 3145728 | tf_op jit(solution)/shard_map/slice | solution.py:19
  105.9 4.4 %slice.282 = f32[1024,384]{0,1:T(8,128)} slice(f32[1024,782]{0,1:T(8,128)S(1)} %maximum_convert_fusion), slice={[0:1024:1], [11:778:2]} | slice | bytes 3145728 | tf_op jit(solution)/shard_map/slice | solution.py:19
  110.2 4.3 %slice.280 = f32[1024,384]{0,1:T(8,128)} slice(f32[1024,782]{0,1:T(8,128)S(1)} %maximum_convert_fusion), slice={[0:1024:1], [10:777:2]} | slice | bytes 3145728 | tf_op jit(solution)/shard_map/slice | solution.py:19
  114.5 4.3 %slice.278 = f32[1024,384]{0,1:T(8,128)} slice(f32[1024,782]{0,1:T(8,128)S(1)} %maximum_convert_fusion), slice={[0:1024:1], [9:776:2]} | slice | bytes 3145728 | tf_op jit(solution)/shard_map/slice | solution.py:19
  118.8 4.2 %slice.276 = f32[1024,384]{0,1:T(8,128)} slice(f32[1024,782]{0,1:T(8,128)S(1)} %maximum_convert_fusion), slice={[0:1024:1], [8:775:2]} | slice | bytes 3145728 | tf_op jit(solution)/shard_map/slice | solution.py:19
  123.0 4.3 %slice.274 = f32[1024,384]{0,1:T(8,128)} slice(f32[1024,782]{0,1:T(8,128)S(1)} %maximum_convert_fusion), slice={[0:1024:1], [7:774:2]} | slice | bytes 3145728 | tf_op jit(solution)/shard_map/slice | solution.py:19
  127.3 4.3 %slice.272 = f32[1024,384]{0,1:T(8,128)} slice(f32[1024,782]{0,1:T(8,128)S(1)} %maximum_convert_fusion), slice={[0:1024:1], [6:773:2]} | slice | bytes 3145728 | tf_op jit(solution)/shard_map/slice | solution.py:19
  131.6 4.3 %slice.270 = f32[1024,384]{0,1:T(8,128)} slice(f32[1024,782]{0,1:T(8,128)S(1)} %maximum_convert_fusion), slice={[0:1024:1], [5:772:2]} | slice | bytes 3145728 | tf_op jit(solution)/shard_map/slice | solution.py:19
  135.9 4.3 %slice.268 = f32[1024,384]{0,1:T(8,128)} slice(f32[1024,782]{0,1:T(8,128)S(1)} %maximum_convert_fusion), slice={[0:1024:1], [4:771:2]} | slice | bytes 3145728 | tf_op jit(solution)/shard_map/slice | solution.py:19
  140.2 4.3 %slice.266 = f32[1024,384]{0,1:T(8,128)} slice(f32[1024,782]{0,1:T(8,128)S(1)} %maximum_convert_fusion), slice={[0:1024:1], [3:770:2]} | slice | bytes 3145728 | tf_op jit(solution)/shard_map/slice | solution.py:19
  144.6 4.3 %slice.264 = f32[1024,384]{0,1:T(8,128)} slice(f32[1024,782]{0,1:T(8,128)S(1)} %maximum_convert_fusion), slice={[0:1024:1], [2:769:2]} | slice | bytes 3145728 | tf_op jit(solution)/shard_map/slice | solution.py:19
  153.1 4.2 %slice.260 = f32[1024,384]{0,1:T(8,128)} slice(f32[1024,782]{0,1:T(8,128)S(1)} %maximum_convert_fusion), slice={[0:1024:1], [0:767:2]} | slice | bytes 3145728 | tf_op jit(solution)/shard_map/slice | solution.py:19
  157.3 21.6 %fusion.38 = (f32[1024]{0:T(1024)S(1)}, f32[1024,384]{0,1:T(8,128)S(1)}) fusion(f32[1024,384]{0,1:T(8,128)} %slice.290, f32[]{:T(128)} %bitcast.15, f32[1024,384]{0,1:T(8,128)} %slice.288, f32[]{:T(128)} %bitcast.14, f32[1024,384]{0,1:T(8,128)} %slice.286, f32[]{:T(128)} %bitcast.13, f32[1024,384]{0,1:T(8,128)} %slice.284, f32[]{:T(128)} %bitcast.12, ...), kind=kLoop, calls=%fused_computation.89 | loop fusion | flops 12581888 | bytes 26742848 | tf_op jit(solution)/shard_map/reduce_sum | solution.py:20
  187.7 5.1 %multiply_bitcast_fusion.3 = f32[8,512,1024]{1,2,0:T(8,128)S(1)} fusion(bf16[8,1024,353]{1,2,0:T(8,128)(2,1)S(1)} %get-tuple-element.15, bf16[512,353]{0,1:T(8,128)(2,1)S(1)} %copy-done.3), kind=kOutput, calls=%fused_computation.4 | convolution fusion | flops 2965372928 | bytes 22922240 | tf_op jit(solution)/shard_map/in,ljn->lij/dot_general | solution.py:43
  192.8 9.0 %multiply_bitcast_fusion = f32[8,512,1024]{1,2,0:T(8,128)} fusion(bf16[8,1024,353]{1,2,0:T(8,128)(2,1)S(1)} %get-tuple-element.16, bf16[512,353]{0,1:T(8,128)(2,1)S(1)} %copy-done.3), kind=kOutput, calls=%fused_computation.1 | convolution fusion | flops 2965372928 | bytes 22922240 | tf_op jit(solution)/shard_map/in,ljn->lij/dot_general | solution.py:43
  201.9 8.5 %multiply_bitcast_fusion.1 = f32[8,512,1024]{1,2,0:T(8,128)} fusion(bf16[8,1024,353]{1,2,0:T(8,128)(2,1)S(1)} %copy-done.1, bf16[512,353]{0,1:T(8,128)(2,1)S(1)} %copy-done.3), kind=kOutput, calls=%fused_computation.2 | convolution fusion | flops 2965372928 | bytes 22922240 | tf_op jit(solution)/shard_map/in,ljn->lij/dot_general | solution.py:43
  210.4 8.5 %multiply_bitcast_fusion.2 = f32[8,512,1024]{1,2,0:T(8,128)} fusion(bf16[8,1024,353]{1,2,0:T(8,128)(2,1)S(1)} %bitcast.166, bf16[512,353]{0,1:T(8,128)(2,1)S(1)} %copy-done.3), kind=kOutput, calls=%fused_computation.3 | convolution fusion | flops 2965372928 | bytes 22922240 | tf_op jit(solution)/shard_map/in,ljn->lij/dot_general | solution.py:43
  218.8 40.9 %pad_maximum_fusion = f32[32,512,1024]{1,2,0:T(8,128)} fusion(f32[8,512,1024]{1,2,0:T(8,128)} %multiply_bitcast_fusion, f32[8,512,1024]{1,2,0:T(8,128)} %multiply_bitcast_fusion.1, f32[8,512,1024]{1,2,0:T(8,128)} %multiply_bitcast_fusion.2, f32[8,512,1024]{1,2,0:T(8,128)S(1)} %multiply_bitcast_fusion.3), kind=kLoop, calls=%fused_computation | loop fusion | flops 50331648 | bytes 134217728 | tf_op jit(solution)/shard_map/concatenate | solution.py:45
  259.7 65.8 %copy.3 = f32[32,512,1024]{2,1,0:T(8,128)} copy(f32[32,512,1024]{1,2,0:T(8,128)} %pad_maximum_fusion) | data formatting | bytes 134217728 | tf_op jit(solution)/shard_map/concatenate | solution.py:45
  (54 shorter events, 58.5 us)
Async XLA Ops:
  6.5 80.3 %all-reduce.3.cloned.1.call-start = ((), (), s32[]{:S(2)}) async-start(), calls=%async_computation | async-start | bytes 3211264 | tf_op jit(solution)/shard_map/psum | solution.py:12
  48.4 19.8 %copy-start.4 = (f32[16]{0:T(128)S(1)}, f32[16]{0:T(128)}, u32[]{:S(2)}) copy-start(f32[16]{0:T(128)} %param.3) | copy-start | bytes 196
  181.7 5.9 %copy-start.3 = (bf16[512,353]{0,1:T(8,128)(2,1)S(1)}, bf16[512,353]{0,1:T(8,128)(2,1)}, u32[]{:S(2)}) copy-start(bf16[512,353]{0,1:T(8,128)(2,1)} %fusion.24) | copy-start | bytes 1084420
  182.5 2.6 copy-start
  185.1 2.5 copy-start.2
  192.8 9.1 %copy-start.1 = (bf16[8,1024,353]{1,2,0:T(8,128)(2,1)S(1)}, bf16[8,1024,353]{1,2,0:T(8,128)(2,1)}, u32[]{:S(2)}) copy-start(bf16[8,1024,353]{1,2,0:T(8,128)(2,1)} %copy-done) | copy-start | bytes 17350660
  192.8 17.5 %slice-start = ((s8[5898240]{0:T(1024)(128)(4,1)}), s8[1703936]{0:T(1024)(128)(4,1)S(1)}, s32[]{:S(2)}) async-start(s8[5898240]{0:T(1024)(128)(4,1)} %bitcast.165), calls=%async_computation.1 | async-start | bytes 3407872
  201.9 8.5 %slice-start.1 = ((s8[5898240]{0:T(1024)(128)(4,1)}), s8[4194304]{0:T(1024)(128)(4,1)S(1)}, s32[]{:S(2)}) async-start(s8[5898240]{0:T(1024)(128)(4,1)} %bitcast.165), calls=%async_computation.2 | async-start | bytes 8388608
Sparse Core Ops, SparseCore 0:
  28.8 58.0 all-reduce.2
where the time goes:
time: 334 us; the launch traced here: 332 us
  local copies, waits for them, and re-layouts  183 us (55%)
  other arithmetic  82.7 us (25%)
  matrix products  31.1 us (9%)
  blocking collectives  20.8 us (6%)
  between operations  13.6 us (4%)
    slice x33, local copies, waits for them, and re-layouts, whiten(): decimated = decimated + taps[k] * samples[:, k:k + 2 * count - 1:2]  109 us
    concatenate x1, local copies, waits for them, and re-layouts, on_device(): return jnp.concatenate(groups, axis=0)  65.8 us
    concatenate x1, other arithmetic, on_device(): return jnp.concatenate(groups, axis=0)  40.9 us
    reduce_sum x2, other arithmetic, whiten(): centred = decimated - jnp.mean(decimated, axis=1, keepdims=True)  37.2 us
    dot_general x4, matrix products, on_device(): jnp.einsum('in,ljn->lij', left, shifted, preferred_element_type=jnp.float32)  31.1 us
    all_gather x1, blocking collectives, on_device(): source = lax.all_gather(traces, 'col', axis=0, tiled=True)  20.8 us
    unnamed x21, local copies, waits for them, and re-layouts  7.78 us
  transfers between devices with their start and end apart: 1, of which 1 were waited for; matrix products, arithmetic and copies ran while one was open for 17% of the time, Pallas kernels for 0%

commit v1 on v0

--- a/solution.py
+++ b/solution.py
@@ -26,7 +26,14 @@
     count = (traces.shape[1] - taps.shape[0] + 2) // 2
     factor = lax.axis_size("row") // lax.axis_size("col")
     column = lax.axis_index("col")
-    source = lax.all_gather(traces, "col", axis=0, tiled=True)
+    ways, here, step = (lax.axis_size("col"), lax.axis_index("col"), traces.shape[0])
+    line, have = (traces, 1)
+    while have < ways:
+        line = jnp.concatenate(
+            [line, lax.ppermute(line, "col", [(d, (d - have) % ways) for d in range(ways)])], axis=0
+        )
+        have = 2 * have
+    source = jnp.roll(line, here * step, axis=0)
     first_block = whiten(source, taps, count)
     pieces = [from_root(source, "row", factor * column + k) for k in range(factor)]
     second_block = jnp.concatenate(pieces, axis=0)

time: 334 us -> 386 us (1.16)
  waiting for transfers between devices: 1.4 us -> 62.4 us
  blocking collectives: 20.8 us -> 0 us
  starting transfers between devices: 0.01 us -> 6.48 us
  local copies, waits for them, and re-layouts: 183 us -> 187 us
    psum x1, waiting for transfers between devices: 1.39 us -> 42.5 us  [from_root(): return lax.psum(jnp.where(mine, array, jnp.zeros_like(array)), axis)]
    all_gather x1 -> x0, blocking collectives: 20.8 us -> none  [on_device(): source = lax.all_gather(traces, 'col', axis=0, tiled=True)]
    ppermute x0 -> x2, waiting for transfers between devices: none -> 19.8 us  [on_device(): lax.ppermute(line, 'col', [(d, (d - have) % ways) for d in range(ways)])]
    ppermute x0 -> x2, starting transfers between devices: none -> 6.48 us  [on_device(): lax.ppermute(line, 'col', [(d, (d - have) % ways) for d in range(ways)])]
    unnamed x21 -> x24, local copies, waits for them, and re-layouts: 7.78 us -> 9.91 us
  transfers between devices with their start and end apart: 1 -> 3, of which waited for: 1 -> 3; matrix products, arithmetic and copies ran while one was open for 17% -> 5% of each run, Pallas kernels for 0% -> 0%
where the time goes in v1:
time: 386 us; the launch traced here: 385 us
  local copies, waits for them, and re-layouts  187 us (48%)
  other arithmetic  84.2 us (22%)
  waiting for transfers between devices  62.4 us (16%)
  matrix products  31.1 us (8%)
  between operations  13.6 us (4%)
  starting transfers between devices  6.48 us (2%)
    slice x33, local copies, waits for them, and re-layouts, whiten(): decimated = decimated + taps[k] * samples[:, k:k + 2 * count - 1:2]  111 us
    concatenate x1, local copies, waits for them, and re-layouts, on_device(): return jnp.concatenate(groups, axis=0)  65.8 us
    psum x1, waiting for transfers between devices, from_root(): return lax.psum(jnp.where(mine, array, jnp.zeros_like(array)), axis)  42.5 us
    concatenate x1, other arithmetic, on_device(): return jnp.concatenate(groups, axis=0)  40.9 us
    reduce_sum x2, other arithmetic, whiten(): centred = decimated - jnp.mean(decimated, axis=1, keepdims=True)  37.5 us
    dot_general x4, matrix products, on_device(): jnp.einsum('in,ljn->lij', left, shifted, preferred_element_type=jnp.float32)  31.1 us
    ppermute x2, waiting for transfers between devices, on_device(): lax.ppermute(line, 'col', [(d, (d - have) % ways) for d in range(ways)])  19.8 us
    unnamed x24, local copies, waits for them, and re-layouts  9.91 us
  transfers between devices with their start and end apart: 3, of which 3 were waited for; matrix products, arithmetic and copies ran while one was open for 5% of the time, Pallas kernels for 0%

profile of v1, /device:TPU:0, one launch (start us, length us, event | category | flops | bytes accessed | tf_op | source)
XLA Modules:
  0.0 384.7 jit_solution(11215123368041567695)
XLA Ops:
  6.5 5.0 %collective-permute-start = (bf16[128,782]{0,1:T(8,128)(2,1)}, bf16[128,782]{0,1:T(8,128)(2,1)S(1)}, u32[]{:S(2)}, u32[]{:S(2)}) collective-permute-start(bf16[128,782]{0,1:T(8,128)(2,1)} %param.2), channel_id=1, source_target_pairs={{0,3},{1,0},{2,1},{3,2},{4,7},{5,4},{6,5},{7,6},{8,11},{9,8},{10,9... | collective-permute-start | bytes 600584 | tf_op jit(solution)/shard_map/ppermute | solution.py:33
  11.6 4.6 %collective-permute-done = bf16[128,782]{0,1:T(8,128)(2,1)S(1)} collective-permute-done((bf16[128,782]{0,1:T(8,128)(2,1)}, bf16[128,782]{0,1:T(8,128)(2,1)S(1)}, u32[]{:S(2)}, u32[]{:S(2)}) %collective-permute-start) | collective-permute-done | bytes 200224 | tf_op jit(solution)/shard_map/ppermute | solution.py:33
  21.6 15.3 %collective-permute-done.1 = bf16[256,782]{0,1:T(8,128)(2,1)S(1)} collective-permute-done((bf16[256,782]{0,1:T(8,128)(2,1)S(1)}, bf16[256,782]{0,1:T(8,128)(2,1)S(1)}, u32[]{:S(2)}, u32[]{:S(2)}) %collective-permute-start.1) | collective-permute-done | bytes 400416 | tf_op jit(solution)/shard_map/ppermute | solution.py:33
  80.3 15.9 %fusion.37 = (f32[512]{0:T(512)S(1)}, f32[512,384]{0,1:T(8,128)S(1)}) fusion(f32[512,384]{0,1:T(8,128)S(1)} %slice.314, f32[]{:T(128)} %bitcast.15, f32[512,384]{0,1:T(8,128)S(1)} %slice.313, f32[]{:T(128)} %bitcast.14, f32[512,384]{0,1:T(8,128)} %slice.312, f32[]{:T(128)} %bitcast.13, f32[512,384]{0,1:T(8,128)} %slice.311, f32[]{:T(128)} %bitcast.12, ...), kind=kLoop, calls=%fused_computation.96 | loop fusion | flops 6290944 | bytes 13371456 | tf_op jit(solution)/shard_map/reduce_sum | solution.py:20
  97.2 42.5 %all-reduce.3.cloned.1.call-done = (bf16[512,782]{0,1:T(8,128)(2,1)}, bf16[512,782]{0,1:T(8,128)(2,1)}) async-done(((bf16[512,782]{0,1:T(8,128)(2,1)}, bf16[512,782]{0,1:T(8,128)(2,1)}), (bf16[512,782]{0,1:T(8,128)(2,1)}, bf16[512,782]{0,1:T(8,128)(2,1)})) %all-reduce.3.cloned.1.call-update) | async-done | bytes 1601552 | tf_op jit(solution)/shard_map/psum | solution.py:12
  141.5 4.3 %slice.290 = f32[1024,384]{0,1:T(8,128)} slice(f32[1024,782]{0,1:T(8,128)S(1)} %maximum_convert_fusion), slice={[0:1024:1], [15:782:2]} | slice | bytes 3145728 | tf_op jit(solution)/shard_map/slice | solution.py:19
  145.8 4.3 %slice.288 = f32[1024,384]{0,1:T(8,128)} slice(f32[1024,782]{0,1:T(8,128)S(1)} %maximum_convert_fusion), slice={[0:1024:1], [14:781:2]} | slice | bytes 3145728 | tf_op jit(solution)/shard_map/slice | solution.py:19
  150.0 4.3 %slice.286 = f32[1024,384]{0,1:T(8,128)} slice(f32[1024,782]{0,1:T(8,128)S(1)} %maximum_convert_fusion), slice={[0:1024:1], [13:780:2]} | slice | bytes 3145728 | tf_op jit(solution)/shard_map/slice | solution.py:19
  154.3 4.3 %slice.284 = f32[1024,384]{0,1:T(8,128)} slice(f32[1024,782]{0,1:T(8,128)S(1)} %maximum_convert_fusion), slice={[0:1024:1], [12:779:2]} | slice | bytes 3145728 | tf_op jit(solution)/shard_map/slice | solution.py:19
  158.6 4.3 %slice.282 = f32[1024,384]{0,1:T(8,128)} slice(f32[1024,782]{0,1:T(8,128)S(1)} %maximum_convert_fusion), slice={[0:1024:1], [11:778:2]} | slice | bytes 3145728 | tf_op jit(solution)/shard_map/slice | solution.py:19
  162.9 4.3 %slice.280 = f32[1024,384]{0,1:T(8,128)} slice(f32[1024,782]{0,1:T(8,128)S(1)} %maximum_convert_fusion), slice={[0:1024:1], [10:777:2]} | slice | bytes 3145728 | tf_op jit(solution)/shard_map/slice | solution.py:19
  175.6 4.2 %slice.274 = f32[1024,384]{0,1:T(8,128)} slice(f32[1024,782]{0,1:T(8,128)S(1)} %maximum_convert_fusion), slice={[0:1024:1], [7:774:2]} | slice | bytes 3145728 | tf_op jit(solution)/shard_map/slice | solution.py:19
  179.8 4.3 %slice.272 = f32[1024,384]{0,1:T(8,128)} slice(f32[1024,782]{0,1:T(8,128)S(1)} %maximum_convert_fusion), slice={[0:1024:1], [6:773:2]} | slice | bytes 3145728 | tf_op jit(solution)/shard_map/slice | solution.py:19
  184.1 4.3 %slice.270 = f32[1024,384]{0,1:T(8,128)} slice(f32[1024,782]{0,1:T(8,128)S(1)} %maximum_convert_fusion), slice={[0:1024:1], [5:772:2]} | slice | bytes 3145728 | tf_op jit(solution)/shard_map/slice | solution.py:19
  188.4 4.3 %slice.268 = f32[1024,384]{0,1:T(8,128)} slice(f32[1024,782]{0,1:T(8,128)S(1)} %maximum_convert_fusion), slice={[0:1024:1], [4:771:2]} | slice | bytes 3145728 | tf_op jit(solution)/shard_map/slice | solution.py:19
  192.7 4.3 %slice.266 = f32[1024,384]{0,1:T(8,128)} slice(f32[1024,782]{0,1:T(8,128)S(1)} %maximum_convert_fusion), slice={[0:1024:1], [3:770:2]} | slice | bytes 3145728 | tf_op jit(solution)/shard_map/slice | solution.py:19
  197.0 4.3 %slice.264 = f32[1024,384]{0,1:T(8,128)} slice(f32[1024,782]{0,1:T(8,128)S(1)} %maximum_convert_fusion), slice={[0:1024:1], [2:769:2]} | slice | bytes 3145728 | tf_op jit(solution)/shard_map/slice | solution.py:19
  209.6 21.6 %fusion.38 = (f32[1024]{0:T(1024)S(1)}, f32[1024,384]{0,1:T(8,128)S(1)}) fusion(f32[1024,384]{0,1:T(8,128)} %slice.290, f32[]{:T(128)} %bitcast.15, f32[1024,384]{0,1:T(8,128)} %slice.288, f32[]{:T(128)} %bitcast.14, f32[1024,384]{0,1:T(8,128)} %slice.286, f32[]{:T(128)} %bitcast.13, f32[1024,384]{0,1:T(8,128)} %slice.284, f32[]{:T(128)} %bitcast.12, ...), kind=kLoop, calls=%fused_computation.97 | loop fusion | flops 12581888 | bytes 26742848 | tf_op jit(solution)/shard_map/reduce_sum | solution.py:20
  240.0 5.1 %multiply_bitcast_fusion.3 = f32[8,512,1024]{1,2,0:T(8,128)S(1)} fusion(bf16[8,1024,353]{1,2,0:T(8,128)(2,1)S(1)} %get-tuple-element.16, bf16[512,353]{0,1:T(8,128)(2,1)S(1)} %copy-done.3), kind=kOutput, calls=%fused_computation.4 | convolution fusion | flops 2965372928 | bytes 22922240 | tf_op jit(solution)/shard_map/in,ljn->lij/dot_general | solution.py:50
  245.1 9.0 %multiply_bitcast_fusion = f32[8,512,1024]{1,2,0:T(8,128)} fusion(bf16[8,1024,353]{1,2,0:T(8,128)(2,1)S(1)} %get-tuple-element.17, bf16[512,353]{0,1:T(8,128)(2,1)S(1)} %copy-done.3), kind=kOutput, calls=%fused_computation.1 | convolution fusion | flops 2965372928 | bytes 22922240 | tf_op jit(solution)/shard_map/in,ljn->lij/dot_general | solution.py:50
  254.2 8.5 %multiply_bitcast_fusion.1 = f32[8,512,1024]{1,2,0:T(8,128)} fusion(bf16[8,1024,353]{1,2,0:T(8,128)(2,1)S(1)} %copy-done.1, bf16[512,353]{0,1:T(8,128)(2,1)S(1)} %copy-done.3), kind=kOutput, calls=%fused_computation.2 | convolution fusion | flops 2965372928 | bytes 22922240 | tf_op jit(solution)/shard_map/in,ljn->lij/dot_general | solution.py:50
  262.7 8.5 %multiply_bitcast_fusion.2 = f32[8,512,1024]{1,2,0:T(8,128)} fusion(bf16[8,1024,353]{1,2,0:T(8,128)(2,1)S(1)} %bitcast.166, bf16[512,353]{0,1:T(8,128)(2,1)S(1)} %copy-done.3), kind=kOutput, calls=%fused_computation.3 | convolution fusion | flops 2965372928 | bytes 22922240 | tf_op jit(solution)/shard_map/in,ljn->lij/dot_general | solution.py:50
  271.1 40.9 %pad_maximum_fusion = f32[32,512,1024]{1,2,0:T(8,128)} fusion(f32[8,512,1024]{1,2,0:T(8,128)} %multiply_bitcast_fusion, f32[8,512,1024]{1,2,0:T(8,128)} %multiply_bitcast_fusion.1, f32[8,512,1024]{1,2,0:T(8,128)} %multiply_bitcast_fusion.2, f32[8,512,1024]{1,2,0:T(8,128)S(1)} %multiply_bitcast_fusion.3), kind=kLoop, calls=%fused_computation | loop fusion | flops 50331648 | bytes 134217728 | tf_op jit(solution)/shard_map/concatenate | solution.py:52
  312.0 65.8 %copy.3 = f32[32,512,1024]{2,1,0:T(8,128)} copy(f32[32,512,1024]{1,2,0:T(8,128)} %pad_maximum_fusion) | data formatting | bytes 134217728 | tf_op jit(solution)/shard_map/concatenate | solution.py:52
  (62 shorter events, 77.0 us)
Async XLA Ops:
  6.5 133.1 %all-reduce.3.cloned.1.call-start = ((), (), s32[]{:S(2)}) async-start(), calls=%async_computation | async-start | bytes 3211264 | tf_op jit(solution)/shard_map/psum | solution.py:12
  6.5 9.6 %collective-permute-start = (bf16[128,782]{0,1:T(8,128)(2,1)}, bf16[128,782]{0,1:T(8,128)(2,1)S(1)}, u32[]{:S(2)}, u32[]{:S(2)}) collective-permute-start(bf16[128,782]{0,1:T(8,128)(2,1)} %param.2), channel_id=1, source_target_pairs={{0,3},{1,0},{2,1},{3,2},{4,7},{5,4},{6,5},{7,6},{8,11},{9,8},{10,9... | collective-permute-start | bytes 600584 | tf_op jit(solution)/shard_map/ppermute | solution.py:33
  17.1 19.7 %collective-permute-start.1 = (bf16[256,782]{0,1:T(8,128)(2,1)S(1)}, bf16[256,782]{0,1:T(8,128)(2,1)S(1)}, u32[]{:S(2)}, u32[]{:S(2)}) collective-permute-start(bf16[256,782]{0,1:T(8,128)(2,1)S(1)} %pad_maximum_fusion.1), channel_id=1, source_target_pairs={{0,2},{1,3},{2,0},{3,1},{4,6},{5,7},{6,4},{7,5},{8,10},{9,11},{10,... | collective-permute-start | bytes 1201160 | tf_op jit(solution)/shard_map/ppermute | solution.py:33
  234.1 5.9 %copy-start.3 = (bf16[512,353]{0,1:T(8,128)(2,1)S(1)}, bf16[512,353]{0,1:T(8,128)(2,1)}, u32[]{:S(2)}) copy-start(bf16[512,353]{0,1:T(8,128)(2,1)} %fusion.24) | copy-start | bytes 1084420
  234.9 2.6 copy-start
  237.4 2.5 copy-start.2
  245.1 9.1 %copy-start.1 = (bf16[8,1024,353]{1,2,0:T(8,128)(2,1)S(1)}, bf16[8,1024,353]{1,2,0:T(8,128)(2,1)}, u32[]{:S(2)}) copy-start(bf16[8,1024,353]{1,2,0:T(8,128)(2,1)} %copy-done) | copy-start | bytes 17350660
  245.1 17.5 %slice-start = ((s8[5898240]{0:T(1024)(128)(4,1)}), s8[1703936]{0:T(1024)(128)(4,1)S(1)}, s32[]{:S(2)}) async-start(s8[5898240]{0:T(1024)(128)(4,1)} %bitcast.165), calls=%async_computation.1 | async-start | bytes 3407872
  254.2 8.5 %slice-start.1 = ((s8[5898240]{0:T(1024)(128)(4,1)}), s8[4194304]{0:T(1024)(128)(4,1)S(1)}, s32[]{:S(2)}) async-start(s8[5898240]{0:T(1024)(128)(4,1)} %bitcast.165), calls=%async_computation.2 | async-start | bytes 8388608
Sparse Core Ops, SparseCore 0:
  80.4 59.2 all-reduce.2
